TPU v7x, 256 devices: a whole 4x4x8 slice. The times are simulated.
256 devices in a mesh: minor: 8 (over z), major: 32 (over y, x, core).
Axes of the slice: x: 4, y: 4, z: 8, core: 2. Of those that a mesh axis runs over, the one named last changes fastest.
Arguments:
- queries: bfloat16 [131072, 1024], P(('major', 'minor')), may hold values from -1.75 to 1.75
- keys: bfloat16 [131072, 1024], P(('major', 'minor')), may hold values from -1.75 to 1.75
- values: bfloat16 [131072, 1024], P(('major', 'minor')), may hold values from -1.75 to 1.75
- cotangent: bfloat16 [131072, 1024], P(('major', 'minor')), may hold values from -1.75 to 1.75
Outputs:
- attended: bfloat16 [131072, 1024], P(('major', 'minor'))
- grad_queries: bfloat16 [131072, 1024], P(('major', 'minor'))
- grad_keys: bfloat16 [131072, 1024], P(('major', 'minor'))
- grad_values: bfloat16 [131072, 1024], P(('major', 'minor'))
All inputs are finite; a program needn't handle non-finite values.
Results may differ from a plain program's by a relative error of at most 0.0057.
Values sent between devices are 32-bit elements; how exact they have to be, the bound alone decides.
A program may use at most 128 MiB of HBM per device.

v0:
```python
import jax
import jax.numpy as jnp
from jax import lax
from jax.sharding import Mesh
from jax.sharding import PartitionSpec as P

H = 16
HD = 64
MAJOR = ("major_0", "major_1", "major_2")
MAJOR_MINOR = ("major_0", "major_1", "major_2", "minor")


def sent_together(arrays, axis, dim, along):
    widths = [a.shape[along] for a in arrays]
    both = jnp.concatenate(arrays, axis=along)
    out = lax.all_gather(both, axis, axis=dim, tiled=True)
    return tuple(jnp.split(out, [sum(widths[:k]) for k in range(1, len(widths))], axis=along))


def neutral_like(value, identity):
    return jnp.zeros_like(value) + jnp.asarray(identity, value.dtype)


def entering(value, axes, combine, identity, reverse):
    before = start = neutral_like(value, identity)
    running = value
    for axis in reversed(axes):
        size, mine = (lax.axis_size(axis), lax.axis_index(axis))
        pieces = lax.all_gather(running, axis)
        inside, running = (start, start)
        for k in reversed(range(size)) if reverse else range(size):
            passed = k > mine if reverse else k < mine
            running = combine(running, pieces[k])
            inside = jnp.where(passed, running, inside)
        before = combine(inside, before)
    return before


def add_pair(first, second):
    return jax.tree.map(lambda a, b: a + b, first, second)


def on_device(queries, keys, values, cotangent):
    rows = queries.shape[0]
    heads = H
    width = HD
    block_index = lax.axis_index(MAJOR) * lax.axis_size("minor") + lax.axis_index("minor")
    pos = (block_index * rows + jnp.arange(rows, dtype=jnp.int32)).astype(jnp.float32)
    scale = 1.0 / jnp.sqrt(pos + 1.0)
    q_heads = queries.reshape(rows, heads, width)
    k_heads = keys.reshape(rows, heads, width)
    v_heads = values.reshape(rows, heads, width)
    g_heads = cotangent.reshape(rows, heads, width)
    q_scaled = (q_heads.astype(jnp.float32) * scale[:, None, None]).astype(jnp.bfloat16)
    s_local = jnp.einsum("thi,thj->hij", k_heads, v_heads, preferred_element_type=jnp.float32)
    r_local = jnp.einsum("thi,thj->hij", q_scaled, g_heads, preferred_element_type=jnp.float32)
    zero = jnp.zeros((heads, width, width), jnp.float32)
    own = lax.axis_index("minor")
    piece = sent_together((s_local[None], r_local[None]), "minor", 0, 1)
    count = piece[0].shape[0]
    index = jnp.arange(count, dtype=jnp.int32)
    before = (index < own).astype(jnp.float32)[:, None, None, None]
    after = (index > own).astype(jnp.float32)[:, None, None, None]
    s_before = jnp.sum(piece[0] * before, 0)
    r_after = jnp.sum(piece[1] * after, 0)
    s_group = jnp.sum(piece[0], 0)
    r_group = jnp.sum(piece[1], 0)
    s_major = entering(s_group, MAJOR, add_pair, zero, False)
    r_major = entering(r_group, MAJOR, add_pair, zero, True)
    s_in = (s_major + s_before).astype(jnp.bfloat16)
    r_in = (r_major + r_after).astype(jnp.bfloat16)
    mask = (jnp.arange(rows)[:, None] >= jnp.arange(rows)[None, :])[None]
    scores = jnp.einsum("thd,shd->hts", q_heads, k_heads, preferred_element_type=jnp.float32)
    weights = jnp.where(mask, scores * scale[None, :, None], 0.0).astype(jnp.bfloat16)
    backs = jnp.einsum("thd,shd->hts", g_heads, v_heads, preferred_element_type=jnp.float32)
    back = jnp.where(mask, backs * scale[None, :, None], 0.0).astype(jnp.bfloat16)
    attended = jnp.einsum("hts,shd->thd", weights, v_heads, preferred_element_type=jnp.float32)
    attended = attended + scale[:, None, None] * jnp.einsum(
        "thi,hij->thj", q_heads, s_in, preferred_element_type=jnp.float32
    )
    grad_q = jnp.einsum("hts,shd->thd", back, k_heads, preferred_element_type=jnp.float32)
    grad_q = grad_q + scale[:, None, None] * jnp.einsum(
        "thj,hij->thi", g_heads, s_in, preferred_element_type=jnp.float32
    )
    grad_k = jnp.einsum("hts,thd->shd", back, q_heads, preferred_element_type=jnp.float32)
    grad_k = grad_k + jnp.einsum("shj,hij->shi", v_heads, r_in, preferred_element_type=jnp.float32)
    grad_v = jnp.einsum("hts,thd->shd", weights, g_heads, preferred_element_type=jnp.float32)
    grad_v = grad_v + jnp.einsum("shi,hij->shj", k_heads, r_in, preferred_element_type=jnp.float32)

    def finish(result):
        return result.reshape(rows, heads * width).astype(jnp.bfloat16)

    return (finish(attended), finish(grad_q), finish(grad_k), finish(grad_v))


def solution(mesh):
    split = Mesh(
        mesh.devices.reshape(mesh.shape["minor"], 4, 4, 2),
        ("minor", "major_0", "major_1", "major_2"),
    )
    placed = (
        P(MAJOR_MINOR, None),
        P(MAJOR_MINOR, None),
        P(MAJOR_MINOR, None),
        P(MAJOR_MINOR, None),
    )
    return jax.shard_map(
        on_device,
        mesh=split,
        in_specs=placed,
        out_specs=(
            P(MAJOR_MINOR, None),
            P(MAJOR_MINOR, None),
            P(MAJOR_MINOR, None),
            P(MAJOR_MINOR, None),
        ),
        check_vma=False,
    )
```

profile of v0, /device:TPU:1, one launch (start us, length us, event | category | flops | bytes accessed | tf_op | source)
XLA Modules:
  0.0 302.7 jit_solution(18433746550468310284)
XLA Ops:
  7.2 0.0 all-gather.10.cloned.1.call-start
  7.2 1.6 copy.40
  8.8 1.3 copy.41
  10.2 1.5 copy.42
  11.7 1.5 copy.43
  13.2 1.6 convolution_bitcast_fusion.1
  14.8 0.4 convolution_bitcast_fusion
  15.2 1.1 pad_maximum_fusion
  16.3 0.0 all-gather.10.cloned.1.call-update
  16.4 0.0 all-gather.16.cloned.1.call-start
  16.4 98.0 %all-gather.10.cloned.1.call-done = f32[8,32,64,64]{3,2,1,0:T(8,128)} async-done(((f32[1,32,64,64]{3,2,1,0:T(8,128)}), f32[8,32,64,64]{3,2,1,0:T(8,128)}) %all-gather.10.cloned.1.call-update) | async-done | bytes 4194320 | tf_op jit(solution)/shard_map/all_gather | solution.py:16
  114.4 6.3 %slice_reduce_fusion = (f32[16,64,64]{2,1,0:T(8,128)}, f32[16,64,64]{2,1,0:T(8,128)}, f32[16,64,64]{2,1,0:T(8,128)}, f32[16,64,64]{2,1,0:T(8,128)S(1)}) fusion(f32[8,32,64,64]{3,2,1,0:T(8,128)} %all-gather.10.cloned.1.call-done, f32[8]{0:T(128)S(1)} %get-tuple-element.21, f32[8]{0:T(128)S(1)} %get-tuple-element.20), kind=kLoop, calls=%fused_computation.4 | loop fusion | flops 2883584 | bytes 5242944 | tf_op jit(solution)/shard_map/reduce_sum | solution.py:67
  120.8 2.8 all-gather
  123.6 1.0 copy-done.3
  124.6 0.9 slice_add_fusion.13
  125.5 0.0 all-gather.16.cloned.1.call-update
  125.5 0.0 all-gather.18.cloned.1.call-start
  125.5 2.8 all-gather.1
  128.3 1.0 copy-done.2
  129.3 0.9 slice_add_fusion.6
  130.1 0.0 all-gather.18.cloned.1.call-update
  130.2 0.0 all-gather.12.cloned.1.call-start
  130.2 27.1 %all-gather.16.cloned.1.call-done = f32[64,64,64]{2,1,0:T(8,128)} async-done(((f32[16,64,64]{2,1,0:T(8,128)}), f32[64,64,64]{2,1,0:T(8,128)}) %all-gather.16.cloned.1.call-update) | async-done | bytes 1048592 | tf_op jit(solution)/shard_map/all_gather | solution.py:29
  157.3 2.5 fusion.16
  159.8 0.2 all-gather.14.cloned.1.call-start
  160.0 0.1 iota_compare_fusion
  160.1 32.5 %all-gather.18.cloned.1.call-done = f32[64,64,64]{2,1,0:T(8,128)} async-done(((f32[16,64,64]{2,1,0:T(8,128)}), f32[64,64,64]{2,1,0:T(8,128)}) %all-gather.18.cloned.1.call-update) | async-done | bytes 1048592 | tf_op jit(solution)/shard_map/all_gather | solution.py:29
  192.6 2.5 fusion.10
  195.1 0.0 all-gather.14.cloned.1.call-update
  195.1 6.4 %select_convert_fusion = bf16[16,512,512]{2,1,0:T(8,128)(2,1)} fusion(bf16[512,16,64]{0,2,1:T(8,128)(2,1)S(1)} %bitcast.98, bf16[512,16,64]{0,2,1:T(8,128)(2,1)S(1)} %bitcast.106, f32[512]{0:T(512)S(1)} %add_rsqrt_fusion, pred[512,512]{1,0:T(8,128)(4,1)S(1)} %iota_compare_fusion), kind=kOutput, calls=%fused_computation | convolution fusion | flops 549453824 | bytes 10749952 | tf_op jit(solution)/shard_map/thd,shd->hts/dot_general | solution.py:75
  201.5 7.6 %select_convert_fusion.1 = bf16[16,512,512]{2,1,0:T(8,128)(2,1)} fusion(bf16[512,16,64]{0,2,1:T(8,128)(2,1)S(1)} %bitcast.102, bf16[512,16,64]{0,2,1:T(8,128)(2,1)} %bitcast.110, f32[512]{0:T(512)S(1)} %add_rsqrt_fusion, pred[512,512]{1,0:T(8,128)(4,1)S(1)} %iota_compare_fusion), kind=kOutput, calls=%fused_computation.1 | convolution fusion | flops 549453824 | bytes 10749952 | tf_op jit(solution)/shard_map/thd,shd->hts/dot_general | solution.py:73
  209.2 18.6 %all-gather.12.cloned.1.call-done = f32[4,16,64,64]{3,2,1,0:T(8,128)} async-done(((f32[1,16,64,64]{3,2,1,0:T(8,128)}), f32[4,16,64,64]{3,2,1,0:T(8,128)}) %all-gather.12.cloned.1.call-update) | async-done | bytes 1048592 | tf_op jit(solution)/shard_map/all_gather | solution.py:29
  227.8 3.3 %fusion.15 = bf16[16,64,64]{2,1,0:T(8,128)(2,1)S(1)} fusion(f32[16,64,64]{2,1,0:T(8,128)} %get-tuple-element.17, f32[4,16,64,64]{3,2,1,0:T(8,128)} %all-gather.12.cloned.1.call-done, f32[64,64,64]{2,1,0:T(8,128)} %all-gather.16.cloned.1.call-done, f32[32,64,64]{2,1,0:T(8,128)} %copy-done.3, pred[]{:T(512)S(6)} %gt.43, pred[]{:T(512)S(6)} %gt.44, ...), kind=kLoop, calls=%fused_computation.38 | loop fusion | flops 1376256 | bytes 3014666 | tf_op jit(solution)/shard_map/convert_element_type | solution.py:70
  231.1 1.8 fusion.18
  232.8 1.8 fusion.17
  234.6 28.2 %all-gather.14.cloned.1.call-done = f32[4,16,64,64]{3,2,1,0:T(8,128)} async-done(((f32[1,16,64,64]{3,2,1,0:T(8,128)}), f32[4,16,64,64]{3,2,1,0:T(8,128)}) %all-gather.14.cloned.1.call-update) | async-done | bytes 1048592 | tf_op jit(solution)/shard_map/all_gather | solution.py:29
  262.9 3.4 %fusion.9 = bf16[16,64,64]{2,1,0:T(8,128)(2,1)S(1)} fusion(f32[16,64,64]{2,1,0:T(8,128)} %get-tuple-element.18, f32[4,16,64,64]{3,2,1,0:T(8,128)} %all-gather.14.cloned.1.call-done, f32[64,64,64]{2,1,0:T(8,128)} %all-gather.18.cloned.1.call-done, f32[32,64,64]{2,1,0:T(8,128)} %copy-done.2, pred[]{:T(512)S(6)} %lt.47, pred[]{:T(512)S(6)} %lt.48, pred[]{:T(512)S(6)} %lt.49, ...), kind=kLoop, calls=%fused_computation.25 | loop fusion | flops 1376256 | bytes 3014666 | tf_op jit(solution)/shard_map/convert_element_type | solution.py:71
  266.3 1.8 fusion.20
  268.1 0.4 fusion.19
  268.5 6.0 %fusion.1 = bf16[512,16,64]{0,2,1:T(8,128)(2,1)} fusion(f32[16,64,512]{2,1,0:T(8,128)S(1)} %fusion.19, bf16[512,16,64]{0,2,1:T(8,128)(2,1)S(1)} %bitcast.104, bf16[16,512,512]{2,1,0:T(8,128)(2,1)} %select_convert_fusion), kind=kOutput, calls=%fused_computation.9 | convolution fusion | flops 537919488 | bytes 12582912 | tf_op jit(solution)/shard_map/hts,thd->shd/dot_general | solution.py:85
  274.5 0.1 copy-done.5
  274.7 3.6 %fusion.2 = bf16[512,16,64]{0,2,1:T(8,128)(2,1)} fusion(f32[16,64,512]{2,1,0:T(8,128)S(1)} %copy-done.5, bf16[16,512,512]{2,1,0:T(8,128)(2,1)S(1)} %bitcast.96, bf16[512,16,64]{0,2,1:T(8,128)(2,1)S(1)} %bitcast.112, f32[512]{0:T(512)S(1)} %add_rsqrt_fusion), kind=kOutput, calls=%fused_computation.11 | convolution fusion | flops 538443776 | bytes 12584960 | tf_op jit(solution)/shard_map/hts,shd->thd/dot_general | solution.py:81
  278.3 2.4 copy.47
  280.6 1.3 copy.48
  281.9 6.8 %fusion.3 = bf16[512,16,64]{0,2,1:T(8,128)(2,1)S(1)} fusion(f32[16,64,512]{2,1,0:T(8,128)} %fusion.17, bf16[16,512,512]{2,1,0:T(8,128)(2,1)} %select_convert_fusion.1, bf16[512,16,64]{0,2,1:T(8,128)(2,1)S(1)} %bitcast.108, f32[512]{0:T(512)S(1)} %add_rsqrt_fusion), kind=kOutput, calls=%fused_computation.13 | convolution fusion | flops 538443776 | bytes 12584960 | tf_op jit(solution)/shard_map/hts,shd->thd/dot_general | solution.py:77
  288.7 4.8 %fusion = bf16[512,16,64]{0,2,1:T(8,128)(2,1)S(1)} fusion(f32[16,64,512]{2,1,0:T(8,128)S(1)} %copy-done, bf16[512,16,64]{0,2,1:T(8,128)(2,1)S(1)} %bitcast.100, bf16[16,512,512]{2,1,0:T(8,128)(2,1)} %select_convert_fusion.1), kind=kOutput, calls=%fused_computation.7 | convolution fusion | flops 537919488 | bytes 12582912 | tf_op jit(solution)/shard_map/hts,thd->shd/dot_general | solution.py:87
  293.5 1.3 copy.49
  294.8 1.3 copy.46
  (19 shorter events, 0.1 us)
Async XLA Ops:
  7.2 1.7 copy-start.6
  7.2 107.3 %all-gather.10.cloned.1.call-start = ((), (), s32[]{:S(2)}) async-start(), calls=%async_computation | async-start | bytes 9437184 | tf_op jit(solution)/shard_map/all_gather | solution.py:16
  16.4 140.9 %all-gather.16.cloned.1.call-start = ((), (), s32[]{:S(2)}) async-start(), calls=%async_computation.3 | async-start | bytes 2621440 | tf_op jit(solution)/shard_map/all_gather | solution.py:29
  123.6 1.0 copy-start.3
  125.5 67.1 %all-gather.18.cloned.1.call-start = ((), (), s32[]{:S(2)}) async-start(), calls=%async_computation.4 | async-start | bytes 2621440 | tf_op jit(solution)/shard_map/all_gather | solution.py:29
  128.3 1.0 copy-start.2
  130.2 97.6 %all-gather.12.cloned.1.call-start = ((), (), s32[]{:S(2)}) async-start(), calls=%async_computation.1 | async-start | bytes 2621440 | tf_op jit(solution)/shard_map/all_gather | solution.py:29
  159.8 103.1 %all-gather.14.cloned.1.call-start = ((), (), s32[]{:S(2)}) async-start(), calls=%async_computation.2 | async-start | bytes 2621440 | tf_op jit(solution)/shard_map/all_gather | solution.py:29
  262.9 3.4 %copy-start.1 = (bf16[512,1024]{0,1:T(8,128)(2,1)S(1)}, bf16[512,1024]{0,1:T(8,128)(2,1)}, u32[]{:S(2)}) copy-start(bf16[512,1024]{0,1:T(8,128)(2,1)} %copy.41) | copy-start | bytes 3145732
  268.1 6.4 %slice-start = ((s8[8388608]{0:T(1024)(128)(4,1)}), s8[4194304]{0:T(1024)(128)(4,1)S(1)}, s32[]{:S(2)}) async-start(s8[8388608]{0:T(1024)(128)(4,1)} %bitcast.95), calls=%async_computation.5 | async-start | bytes 8388608
  268.5 6.0 %slice-start.1 = ((s8[8388608]{0:T(1024)(128)(4,1)}), s8[4194304]{0:T(1024)(128)(4,1)S(1)}, s32[]{:S(2)}) async-start(s8[8388608]{0:T(1024)(128)(4,1)} %bitcast.95), calls=%async_computation.6 | async-start | bytes 8388608
  268.5 6.1 %copy-start.5 = (f32[16,64,512]{2,1,0:T(8,128)S(1)}, f32[16,64,512]{2,1,0:T(8,128)}, u32[]{:S(2)}) copy-start(f32[16,64,512]{2,1,0:T(8,128)} %fusion.18) | copy-start | bytes 6291460
  278.3 2.4 copy-start.4
  281.9 6.8 %copy-start = (f32[16,64,512]{2,1,0:T(8,128)S(1)}, f32[16,64,512]{2,1,0:T(8,128)}, u32[]{:S(2)}) copy-start(f32[16,64,512]{2,1,0:T(8,128)} %fusion.20) | copy-start | bytes 6291460
Sparse Core Ops, SparseCore 0:
  16.5 97.9 all-gather.9
  125.6 31.6 all-gather.15
  159.1 33.4 all-gather.17
  194.2 33.4 all-gather.11
  229.4 33.4 all-gather.13
where the time goes:
time: 303 us
  waiting for transfers between devices  204 us (67%)
  matrix products  43.1 us (14%)
  other arithmetic  20.9 us (7%)
  local copies, waits for them, and re-layouts  14.3 us (5%)
  between operations  13.9 us (5%)
  blocking collectives  5.61 us (2%)
    all_gather x4, waiting for transfers between devices, entering(): pieces = lax.all_gather(running, axis)  106 us
    all_gather x1, waiting for transfers between devices, sent_together(): out = lax.all_gather(both, axis, axis=dim, tiled=True)  98 us
    unnamed x26, local copies, waits for them, and re-layouts  14.3 us
    dot_general x1, matrix products, on_device(): jnp.einsum('thd,shd->hts', q_heads, k_heads, preferred_element_type=jnp.f...  7.63 us
    dot_general x1, matrix products, on_device(): jnp.einsum('hts,shd->thd', weights, v_heads, preferred_element_type=jnp.f...  6.75 us
    add x4, other arithmetic, add_pair(): return jax.tree.map(lambda a, b: a + b, first, second)  6.72 us
    dot_general x1, matrix products, on_device(): jnp.einsum('thd,shd->hts', g_heads, v_heads, preferred_element_type=jnp.f...  6.43 us
    reduce_sum x1, other arithmetic, on_device(): r_group = jnp.sum(piece[1], 0)  6.32 us
  transfers between devices with their start and end apart: 5, of which 5 were waited for; matrix products, arithmetic and copies ran while one was open for 9% of the time, Pallas kernels for 0%

commit v1 on v0

v1 whole, which is shorter than its diff:
```python
import functools

import jax
import jax.numpy as jnp
from jax import lax
from jax.experimental import pallas as pl
from jax.experimental.pallas import tpu as pltpu
from jax.sharding import PartitionSpec as P

TOK = 512
COLS = 1024
PAIRS = 8
CHUNK = 128
CHUNKS = TOK // CHUNK
F32 = jnp.float32
BF16 = jnp.bfloat16
MESH = pl.DeviceIdType.MESH

NT = (((1,), (1,)), ((), ()))
NN = (((1,), (0,)), ((), ()))
TN = (((0,), (0,)), ((), ()))


def dot(a, b, dims):
    return lax.dot_general(a, b, dims, preferred_element_type=F32)


def lanes_of(pair):
    return pl.ds(pl.multiple_of(pair * 128, 128), 128)


def token_scale(block, shape):
    pos = block * TOK + lax.broadcasted_iota(jnp.int32, shape, 0)
    return 1.0 / jnp.sqrt(pos.astype(F32) + 1.0)


def both_heads(x):
    low = lax.broadcasted_iota(jnp.int32, x.shape, 1) < 64
    zero = jnp.zeros_like(x)
    return jnp.concatenate([jnp.where(low, x, zero), jnp.where(low, zero, x)], axis=0)


def diagonal(x):
    row = lax.broadcasted_iota(jnp.int32, x.shape, 0) < 64
    col = lax.broadcasted_iota(jnp.int32, x.shape, 1) < 64
    return jnp.where(row == col, x, jnp.zeros_like(x))


def compact(x):
    low = lax.broadcasted_iota(jnp.int32, (64, 128), 1) < 64
    return jnp.where(low, x[0:64], x[64:128])


def states_kernel(
    q_hbm, k_hbm, v_hbm, g_hbm, part_hbm, state_hbm,
    q, k, v, g, qc, gc, scale, part, send, fwd, total, plane, ret, back,
    in_sem, out_sem, state_sem, fs_sem, fr_sem, ps_sem, pr_sem, rs_sem, rr_sem,
):
    z = lax.axis_index("minor")
    group = lax.axis_index("major")
    core = lax.rem(group, 2)
    chip = group // 2
    mine = core * 8 + z
    owned = z * 2 + core

    def column(step):
        return lax.rem(z + step // 2, 8), lax.rem(core + step % 2, 2)

    loads = [
        pltpu.make_async_copy(src, dst, in_sem.at[i])
        for i, (src, dst) in enumerate(((k_hbm, k), (v_hbm, v), (q_hbm, q), (g_hbm, g)))
    ]
    for load in loads:
        load.start()

    barrier = pltpu.get_barrier_semaphore()
    for step in range(1, 16):
        to_z, to_core = column(step)
        pl.semaphore_signal(
            barrier, inc=1, device_id={"minor": to_z, "major": chip * 2 + to_core}, device_id_type=MESH
        )
        other = lax.rem(chip + step, 16)
        pl.semaphore_signal(
            barrier, inc=1, device_id={"minor": z, "major": other * 2 + core}, device_id_type=MESH
        )

    scale[...] = token_scale(group * 8 + z, (TOK, 128))
    loads[0].wait()
    loads[1].wait()

    def key_states(p, _):
        at = lanes_of(p)
        s = compact(dot(k[:, at], v[:, at], TN))
        send[2 * p, 0:32] = s[0:32]
        send[2 * p + 1, 0:32] = s[32:64]
        return 0

    lax.fori_loop(0, PAIRS, key_states, 0)
    loads[2].wait()
    loads[3].wait()

    def query_states(p, _):
        at = lanes_of(p)
        c = scale[...]
        scaled = (q[:, at].astype(F32) * c).astype(BF16)
        qc[:, at] = scaled
        gc[:, at] = (g[:, at].astype(F32) * c).astype(BF16)
        r = compact(dot(scaled, g[:, at], TN))
        send[2 * p, 32:64] = r[0:32]
        send[2 * p + 1, 32:64] = r[32:64]
        return 0

    lax.fori_loop(0, PAIRS, query_states, 0)
    pl.semaphore_wait(barrier, 30)

    def forward(step):
        to_z, to_core = column(step)
        return pltpu.make_async_remote_copy(
            src_ref=send.at[to_z * 2 + to_core],
            dst_ref=fwd.at[mine],
            send_sem=fs_sem.at[step],
            recv_sem=fr_sem.at[mine],
            device_id={"minor": to_z, "major": chip * 2 + to_core},
            device_id_type=MESH,
        )

    def landed(step):
        from_z, from_core = column(step)
        slot = from_core * 8 + from_z
        return pltpu.make_async_remote_copy(
            src_ref=send.at[0],
            dst_ref=fwd.at[slot],
            send_sem=fs_sem.at[step],
            recv_sem=fr_sem.at[slot],
            device_id={"minor": from_z, "major": chip * 2 + from_core},
            device_id_type=MESH,
        )

    for step in range(1, 16):
        forward(step).start()
    fwd[mine] = send[owned]

    def inside(p, _):
        at = lanes_of(p)
        causal = lax.broadcasted_iota(jnp.int32, (CHUNK, 2 * CHUNK), 0) >= (
            lax.broadcasted_iota(jnp.int32, (CHUNK, 2 * CHUNK), 1) % CHUNK
        )
        state = None
        adjoints = []
        for n in range(CHUNKS):
            rows = pl.ds(n * CHUNK, CHUNK)
            adjoints.append(dot(qc[rows, at], g[rows, at], TN) if n else None)
        later = [None] * CHUNKS
        running = None
        for n in reversed(range(1, CHUNKS)):
            running = adjoints[n] if running is None else running + adjoints[n]
            later[n - 1] = running
        for n in range(CHUNKS):
            rows = pl.ds(n * CHUNK, CHUNK)
            q_n, k_n, v_n, g_n = q[rows, at], k[rows, at], v[rows, at], g[rows, at]
            qc_n, gc_n = qc[rows, at], gc[rows, at]
            k_two, v_two = both_heads(k_n), both_heads(v_n)
            q_two, g_two = both_heads(q_n), both_heads(g_n)
            weights = jnp.where(causal, dot(qc_n, k_two, NT), 0.0).astype(BF16)
            backs = jnp.where(causal, dot(gc_n, v_two, NT), 0.0).astype(BF16)
            w_rows = jnp.concatenate([weights[:, :CHUNK], weights[:, CHUNK:]], axis=0)
            b_rows = jnp.concatenate([backs[:, :CHUNK], backs[:, CHUNK:]], axis=0)
            attended = dot(weights, v_two, NN)
            grad_q = dot(backs, k_two, NN)
            grad_k = dot(b_rows, q_two, TN)
            grad_v = dot(w_rows, g_two, TN)
            if n:
                s = diagonal(state).astype(BF16)
                attended = attended + dot(qc_n, s, NN)
                grad_q = grad_q + dot(gc_n, s, NT)
            if n < CHUNKS - 1:
                r = diagonal(later[n]).astype(BF16)
                grad_k = grad_k + dot(v_n, r, NT)
                grad_v = grad_v + dot(k_n, r, NN)
                more = dot(k_n, v_n, TN)
                state = more if state is None else state + more
            for i, x in enumerate((attended, grad_q, grad_k, grad_v)):
                part[p, i, rows] = x
        pltpu.make_async_copy(part.at[p], part_hbm.at[p], out_sem.at[p]).start()
        return 0

    lax.fori_loop(0, 4, inside, 0)

    for step in range(1, 16):
        landed(step).wait_recv()
    run = jnp.zeros((32, 128), F32)
    for d in range(16):
        ret[d, 0:32] = run
        run = run + fwd[d, 0:32]
    total[0] = run
    run = jnp.zeros((32, 128), F32)
    for d in reversed(range(16)):
        ret[d, 32:64] = run
        run = run + fwd[d, 32:64]
    total[1] = run

    def across(step):
        other = lax.rem(chip + step, 16)
        return pltpu.make_async_remote_copy(
            src_ref=total.at[jnp.where(other > chip, 0, 1)],
            dst_ref=plane.at[chip],
            send_sem=ps_sem.at[step],
            recv_sem=pr_sem.at[chip],
            device_id={"minor": z, "major": other * 2 + core},
            device_id_type=MESH,
        )

    def crossed(step):
        other = lax.rem(chip + step, 16)
        return pltpu.make_async_remote_copy(
            src_ref=total.at[0],
            dst_ref=plane.at[other],
            send_sem=ps_sem.at[step],
            recv_sem=pr_sem.at[other],
            device_id={"minor": z, "major": other * 2 + core},
            device_id_type=MESH,
        )

    for step in range(1, 16):
        across(step).start()
    plane[chip] = jnp.zeros((32, 128), F32)

    lax.fori_loop(4, 6, inside, 0)

    for step in range(1, 16):
        crossed(step).wait_recv()
    before = jnp.zeros((32, 128), F32)
    after = jnp.zeros((32, 128), F32)
    for n in range(16):
        piece = plane[n]
        before = before + jnp.where(n < chip, piece, 0.0)
        after = after + jnp.where(n > chip, piece, 0.0)
    for d in range(16):
        ret[d, 0:32] = ret[d, 0:32] + before
        ret[d, 32:64] = ret[d, 32:64] + after

    def returned(step):
        to_z, to_core = column(step)
        return pltpu.make_async_remote_copy(
            src_ref=ret.at[to_core * 8 + to_z],
            dst_ref=back.at[owned],
            send_sem=rs_sem.at[step],
            recv_sem=rr_sem.at[owned],
            device_id={"minor": to_z, "major": chip * 2 + to_core},
            device_id_type=MESH,
        )

    def arrived(step):
        from_z, from_core = column(step)
        slot = from_z * 2 + from_core
        return pltpu.make_async_remote_copy(
            src_ref=ret.at[0],
            dst_ref=back.at[slot],
            send_sem=rs_sem.at[step],
            recv_sem=rr_sem.at[slot],
            device_id={"minor": from_z, "major": chip * 2 + from_core},
            device_id_type=MESH,
        )

    for step in range(1, 16):
        returned(step).start()
    back[owned] = ret[mine]

    lax.fori_loop(6, 8, inside, 0)

    for step in range(1, 16):
        arrived(step).wait_recv()
    out = pltpu.make_async_copy(back, state_hbm, state_sem)
    out.start()
    for step in range(1, 16):
        forward(step).wait_send()
        across(step).wait_send()
        returned(step).wait_send()

    def stored(p, _):
        pltpu.make_async_copy(part.at[p], part_hbm.at[p], out_sem.at[p]).wait()
        return 0

    lax.fori_loop(0, PAIRS, stored, 0)
    out.wait()


def finish_kernel(q, k, v, g, part, state, attended, grad_q, grad_k, grad_v):
    block = lax.axis_index("major") * 8 + lax.axis_index("minor")
    c = token_scale(block, (TOK, 128))
    s = jnp.concatenate([state[0, 0:32], state[1, 0:32]] * 2, axis=0)
    r = jnp.concatenate([state[0, 32:64], state[1, 32:64]] * 2, axis=0)
    s = diagonal(s).astype(BF16)
    r = diagonal(r).astype(BF16)
    attended[...] = (part[0, 0] + c * dot(q[...], s, NN)).astype(BF16)
    grad_q[...] = (part[0, 1] + c * dot(g[...], s, NT)).astype(BF16)
    grad_k[...] = (part[0, 2] + dot(v[...], r, NT)).astype(BF16)
    grad_v[...] = (part[0, 3] + dot(k[...], r, NN)).astype(BF16)


def on_device(queries, keys, values, cotangent):
    hbm = pl.BlockSpec(memory_space=pl.ANY)
    dma = pltpu.SemaphoreType.DMA
    part, state = pl.pallas_call(
        states_kernel,
        name="states",
        out_shape=(
            jax.ShapeDtypeStruct((PAIRS, 4, TOK, 128), F32),
            jax.ShapeDtypeStruct((16, 64, 128), F32),
        ),
        in_specs=[hbm] * 4,
        out_specs=(hbm, hbm),
        scratch_shapes=[
            pltpu.VMEM((TOK, COLS), BF16),
            pltpu.VMEM((TOK, COLS), BF16),
            pltpu.VMEM((TOK, COLS), BF16),
            pltpu.VMEM((TOK, COLS), BF16),
            pltpu.VMEM((TOK, COLS), BF16),
            pltpu.VMEM((TOK, COLS), BF16),
            pltpu.VMEM((TOK, 128), F32),
            pltpu.VMEM((PAIRS, 4, TOK, 128), F32),
            pltpu.VMEM((16, 64, 128), F32),
            pltpu.VMEM((16, 64, 128), F32),
            pltpu.VMEM((2, 32, 128), F32),
            pltpu.VMEM((16, 32, 128), F32),
            pltpu.VMEM((16, 64, 128), F32),
            pltpu.VMEM((16, 64, 128), F32),
            dma((4,)),
            dma((PAIRS,)),
            dma,
            dma((16,)),
            dma((16,)),
            dma((16,)),
            dma((16,)),
            dma((16,)),
            dma((16,)),
        ],
        compiler_params=pltpu.CompilerParams(
            collective_id=0, has_side_effects=True, vmem_limit_bytes=40 << 20
        ),
    )(queries, keys, values, cotangent)
    cols = pl.BlockSpec((TOK, 128), lambda p: (0, p))
    out = jax.ShapeDtypeStruct((TOK, COLS), BF16)
    return pl.pallas_call(
        finish_kernel,
        name="finish",
        grid=(PAIRS,),
        out_shape=(out,) * 4,
        in_specs=[cols] * 4
        + [
            pl.BlockSpec((1, 4, TOK, 128), lambda p: (p, 0, 0, 0)),
            pl.BlockSpec((2, 64, 128), lambda p: (p, 0, 0)),
        ],
        out_specs=(cols,) * 4,
        compiler_params=pltpu.CompilerParams(vmem_limit_bytes=40 << 20),
    )(queries, keys, values, cotangent, part, state)


def solution(mesh):
    placed = P(("major", "minor"), None)
    return jax.shard_map(
        on_device, mesh=mesh, in_specs=(placed,) * 4, out_specs=(placed,) * 4, check_vma=False
    )
```

time: 303 us -> 56.1 us (0.19)
  waiting for transfers between devices: 204 us -> 0 us
  Pallas kernels: 0 us -> 50.4 us
  matrix products: 43.1 us -> 0 us
  other arithmetic: 20.9 us -> 0 us
  between operations: 13.9 us -> 0.65 us
  local copies, waits for them, and re-layouts: 14.3 us -> 4.89 us
  blocking collectives: 5.61 us -> 0 us
    all_gather x5 -> x0, waiting for transfers between devices: 204 us -> none  [the longest x4 106 us: entering(): pieces = lax.all_gather(running, axis)]
    pallas_call x0 -> x2, Pallas kernels: none -> 50.4 us  [the longest x1 45.2 us: on_device(): pl.pallas_call(states_kernel, name='states', out_shape=(jax.ShapeDtypeStr...]
    dot_general x12 -> x0, matrix products: 43.1 us -> none  [the longest x1 7.63 us: on_device(): jnp.einsum('thd,shd->hts', q_heads, k_heads, preferred_element_type=jnp.f...]
    unnamed x26 -> x8, local copies, waits for them, and re-layouts: 14.3 us -> 4.89 us
    add x4 -> x0, other arithmetic: 6.72 us -> none  [add_pair(): return jax.tree.map(lambda a, b: a + b, first, second)]
    convert_element_type x3 -> x0, other arithmetic: 6.69 us -> none  [the longest x1 3.38 us: on_device(): r_in = (r_major + r_after).astype(jnp.bfloat16)]
    reduce_sum x1 -> x0, other arithmetic: 6.32 us -> none  [on_device(): r_group = jnp.sum(piece[1], 0)]
    all_gather x2 -> x0, blocking collectives: 5.61 us -> none  [entering(): pieces = lax.all_gather(running, axis)]
  transfers between devices with their start and end apart: 5 -> 0, of which waited for: 5 -> 0; matrix products, arithmetic and copies ran while one was open for 9% -> 0% of each run, Pallas kernels for 0% -> 0%
where the time goes in v1:
time: 56.1 us; the launch traced here: 55.9 us
  Pallas kernels  50.4 us (90%)
  local copies, waits for them, and re-layouts  4.89 us (9%)
  between operations  0.65 us (1%)
    pallas_call x1, Pallas kernels, on_device(): pl.pallas_call(states_kernel, name='states', out_shape=(jax.ShapeDtypeStr...  45.2 us
    pallas_call x1, Pallas kernels, on_device(): pl.pallas_call(finish_kernel, name='finish', grid=(PAIRS,), out_shape=(ou...  5.17 us
    unnamed x8, local copies, waits for them, and re-layouts  4.89 us

profile of v1, /device:TPU:1, one launch (start us, length us, event | category | flops | bytes accessed | tf_op | source)
XLA Modules:
  0.0 55.9 jit_solution(3593016035730318930)
XLA Ops:
  0.6 0.0 copy-start
  0.6 1.2 %copy-done = bf16[512,1024]{1,0:T(8,128)(2,1)S(1)} copy-done((bf16[512,1024]{1,0:T(8,128)(2,1)S(1)}, bf16[512,1024]{1,0:T(8,128)(2,1)}, u32[]{:S(2)}) %copy-start) | copy-done | bytes 1048600
  1.9 0.0 copy-start.1
  1.9 1.2 %copy-done.1 = bf16[512,1024]{1,0:T(8,128)(2,1)S(1)} copy-done((bf16[512,1024]{1,0:T(8,128)(2,1)S(1)}, bf16[512,1024]{1,0:T(8,128)(2,1)}, u32[]{:S(2)}) %copy-start.1) | copy-done | bytes 1048600
  3.1 0.0 copy-start.2
  3.1 1.2 %copy-done.2 = bf16[512,1024]{1,0:T(8,128)(2,1)S(1)} copy-done((bf16[512,1024]{1,0:T(8,128)(2,1)S(1)}, bf16[512,1024]{1,0:T(8,128)(2,1)}, u32[]{:S(2)}) %copy-start.2) | copy-done | bytes 1048600
  4.3 0.0 copy-start.3
  4.3 1.2 %copy-done.3 = bf16[512,1024]{1,0:T(8,128)(2,1)S(1)} copy-done((bf16[512,1024]{1,0:T(8,128)(2,1)S(1)}, bf16[512,1024]{1,0:T(8,128)(2,1)}, u32[]{:S(2)}) %copy-start.3) | copy-done | bytes 1048600
  5.5 45.2 %states.1 = (f32[8,4,512,128]{3,2,1,0:T(8,128)S(1)}, f32[16,64,128]{2,1,0:T(8,128)S(1)}) custom-call(bf16[512,1024]{1,0:T(8,128)(2,1)S(1)} %copy-done, bf16[512,1024]{1,0:T(8,128)(2,1)S(1)} %copy-done.1, bf16[512,1024]{1,0:T(8,128)(2,1)S(1)} %copy-done.2, bf16[512,1024]{1,0:T(8,128)(2,1)S(1)} %copy-done.3), custom_call_target="tpu_custom_call" | custom-call | tf_op jit(solution)/shard_map/states/pallas_call | solution.py:304
  50.7 5.2 %finish.1 = (bf16[512,1024]{1,0:T(8,128)(2,1)}, bf16[512,1024]{1,0:T(8,128)(2,1)}, bf16[512,1024]{1,0:T(8,128)(2,1)}, bf16[512,1024]{1,0:T(8,128)(2,1)}) custom-call(bf16[512,1024]{1,0:T(8,128)(2,1)S(1)} %copy-done, bf16[512,1024]{1,0:T(8,128)(2,1)S(1)} %copy-done.1, bf16[512,1024]{1,0:T(8,128)(2,1)S(1)} %copy-done.2, bf16[512,1024]{1,0:T(8,128)(2,1)S(1)} %copy-done.3, ...), custom_call_target="tpu_custom_call" | custom-call | tf_op jit(solution)/shard_map/finish/pallas_call | solution.py:344
Async XLA Ops:
  0.6 1.2 %copy-start = (bf16[512,1024]{1,0:T(8,128)(2,1)S(1)}, bf16[512,1024]{1,0:T(8,128)(2,1)}, u32[]{:S(2)}) copy-start(bf16[512,1024]{1,0:T(8,128)(2,1)} %q.1) | copy-start | bytes 3145732
  1.9 1.2 %copy-start.1 = (bf16[512,1024]{1,0:T(8,128)(2,1)S(1)}, bf16[512,1024]{1,0:T(8,128)(2,1)}, u32[]{:S(2)}) copy-start(bf16[512,1024]{1,0:T(8,128)(2,1)} %k.1) | copy-start | bytes 3145732
  3.1 1.2 %copy-start.2 = (bf16[512,1024]{1,0:T(8,128)(2,1)S(1)}, bf16[512,1024]{1,0:T(8,128)(2,1)}, u32[]{:S(2)}) copy-start(bf16[512,1024]{1,0:T(8,128)(2,1)} %v.1) | copy-start | bytes 3145732
  4.3 1.2 %copy-start.3 = (bf16[512,1024]{1,0:T(8,128)(2,1)S(1)}, bf16[512,1024]{1,0:T(8,128)(2,1)}, u32[]{:S(2)}) copy-start(bf16[512,1024]{1,0:T(8,128)(2,1)} %g.1) | copy-start | bytes 3145732

commit v2 on v1

v2 whole, which is shorter than its diff:
```python
import jax
import jax.numpy as jnp
from jax import lax
from jax.experimental import pallas as pl
from jax.experimental.pallas import tpu as pltpu
from jax.sharding import PartitionSpec as P

TOK = 512
COLS = 1024
PAIRS = 8
CHUNK = 128
CHUNKS = TOK // CHUNK
F32 = jnp.float32
BF16 = jnp.bfloat16
MESH = pl.DeviceIdType.MESH

NT = (((1,), (1,)), ((), ()))
NN = (((1,), (0,)), ((), ()))
TN = (((0,), (0,)), ((), ()))


def dot(a, b, dims):
    return lax.dot_general(a, b, dims, preferred_element_type=F32)


def lanes_of(pair):
    return pl.ds(pl.multiple_of(pair * 128, 128), 128)


def token_scale(block, shape):
    pos = block * TOK + lax.broadcasted_iota(jnp.int32, shape, 0)
    return 1.0 / jnp.sqrt(pos.astype(F32) + 1.0)


def both_heads(x):
    low = lax.broadcasted_iota(jnp.int32, x.shape, 1) < 64
    zero = jnp.zeros_like(x)
    return jnp.concatenate([jnp.where(low, x, zero), jnp.where(low, zero, x)], axis=0)


def diagonal(x):
    row = lax.broadcasted_iota(jnp.int32, x.shape, 0) < 64
    col = lax.broadcasted_iota(jnp.int32, x.shape, 1) < 64
    return jnp.where(row == col, x, jnp.zeros_like(x))


def compact(x):
    low = lax.broadcasted_iota(jnp.int32, (64, 128), 1) < 64
    return jnp.where(low, x[0:64], x[64:128])


def attention_kernel(
    q_hbm, k_hbm, v_hbm, g_hbm, attended, grad_q, grad_k, grad_v,
    q, k, v, g, qc, gc, scale, part, send, fwd, total, plane, ret, back,
    in_sem, fs_sem, fr_sem, ps_sem, pr_sem, rs_sem, rr_sem,
):
    z = lax.axis_index("minor")
    group = lax.axis_index("major")
    core = lax.rem(group, 2)
    chip = group // 2
    mine = core * 8 + z
    owned = z * 2 + core
    zeros = jnp.zeros((32, 128), F32)

    def column(step):
        return lax.rem(z + step // 2, 8), lax.rem(core + step % 2, 2)

    loads = [
        pltpu.make_async_copy(src, dst, in_sem.at[i])
        for i, (src, dst) in enumerate(((k_hbm, k), (v_hbm, v), (q_hbm, q), (g_hbm, g)))
    ]
    for load in loads:
        load.start()

    barrier = pltpu.get_barrier_semaphore()
    for step in range(1, 16):
        to_z, to_core = column(step)
        pl.semaphore_signal(
            barrier, inc=1, device_id={"minor": to_z, "major": chip * 2 + to_core}, device_id_type=MESH
        )
        other = lax.rem(chip + step, 16)
        pl.semaphore_signal(
            barrier, inc=1, device_id={"minor": z, "major": other * 2 + core}, device_id_type=MESH
        )

    def forward(kind, step, peer):
        to_z, to_core = column(step)
        slot = to_core * 8 + to_z if peer else mine
        return pltpu.make_async_remote_copy(
            src_ref=send.at[kind, to_z * 2 + to_core],
            dst_ref=fwd.at[kind, slot],
            send_sem=fs_sem.at[kind, step],
            recv_sem=fr_sem.at[kind, slot],
            device_id={"minor": to_z, "major": chip * 2 + to_core},
            device_id_type=MESH,
        )

    def across(kind, step, peer):
        other = lax.rem(chip + step, 16)
        slot = other if peer else chip
        return pltpu.make_async_remote_copy(
            src_ref=total.at[kind],
            dst_ref=plane.at[kind, slot],
            send_sem=ps_sem.at[kind, step],
            recv_sem=pr_sem.at[kind, slot],
            device_id={"minor": z, "major": other * 2 + core},
            device_id_type=MESH,
        )

    def returned(kind, step, peer):
        to_z, to_core = column(step)
        slot = to_z * 2 + to_core if peer else owned
        return pltpu.make_async_remote_copy(
            src_ref=ret.at[kind, to_core * 8 + to_z],
            dst_ref=back.at[kind, slot],
            send_sem=rs_sem.at[kind, step],
            recv_sem=rr_sem.at[kind, slot],
            device_id={"minor": to_z, "major": chip * 2 + to_core},
            device_id_type=MESH,
        )

    def ahead(kind, step):
        other = lax.rem(chip + step, 16)
        return other > chip if kind == 0 else other < chip

    def send_slices(kind):
        for step in range(1, 16):
            forward(kind, step, False).start()
        fwd[kind, mine] = send[kind, owned]

    def add_column(kind):
        for step in range(1, 16):
            forward(kind, step, True).wait_recv()
        run = zeros
        for d in range(16) if kind == 0 else reversed(range(16)):
            ret[kind, d] = run
            run = run + fwd[kind, d]
        total[kind] = run
        for step in range(1, 16):
            pl.when(ahead(kind, step))(across(kind, step, False).start)

    def add_plane(kind):
        for step in range(1, 16):
            pl.when(ahead(1 - kind, step))(across(kind, step, True).wait_recv)
        entering = zeros
        for n in range(16):
            passed = n < chip if kind == 0 else n > chip
            entering = entering + jnp.where(passed, plane[kind, n], 0.0)
        for d in range(16):
            ret[kind, d] = ret[kind, d] + entering
        for step in range(1, 16):
            returned(kind, step, False).start()
        back[kind, owned] = ret[kind, mine]

    scale[...] = token_scale(group * 8 + z, (TOK, 128))
    loads[0].wait()
    loads[1].wait()

    def key_states(p, _):
        at = lanes_of(p)
        s = compact(dot(k[:, at], v[:, at], TN))
        send[0, 2 * p] = s[0:32]
        send[0, 2 * p + 1] = s[32:64]
        return 0

    lax.fori_loop(0, PAIRS, key_states, 0)
    pl.semaphore_wait(barrier, 30)
    send_slices(0)
    loads[2].wait()
    loads[3].wait()

    def query_states(p, _):
        at = lanes_of(p)
        c = scale[...]
        scaled = (q[:, at].astype(F32) * c).astype(BF16)
        qc[:, at] = scaled
        gc[:, at] = (g[:, at].astype(F32) * c).astype(BF16)
        r = compact(dot(scaled, g[:, at], TN))
        send[1, 2 * p] = r[0:32]
        send[1, 2 * p + 1] = r[32:64]
        return 0

    lax.fori_loop(0, PAIRS, query_states, 0)
    send_slices(1)

    def inside(p, _):
        at = lanes_of(p)
        causal = lax.broadcasted_iota(jnp.int32, (CHUNK, 2 * CHUNK), 0) >= (
            lax.broadcasted_iota(jnp.int32, (CHUNK, 2 * CHUNK), 1) % CHUNK
        )
        state = None
        later = [None] * CHUNKS
        running = None
        for n in reversed(range(1, CHUNKS)):
            rows = pl.ds(n * CHUNK, CHUNK)
            more = dot(qc[rows, at], g[rows, at], TN)
            running = more if running is None else running + more
            later[n - 1] = running
        for n in range(CHUNKS):
            rows = pl.ds(n * CHUNK, CHUNK)
            q_n, k_n, v_n, g_n = q[rows, at], k[rows, at], v[rows, at], g[rows, at]
            qc_n, gc_n = qc[rows, at], gc[rows, at]
            k_two, v_two = both_heads(k_n), both_heads(v_n)
            q_two, g_two = both_heads(q_n), both_heads(g_n)
            weights = jnp.where(causal, dot(qc_n, k_two, NT), 0.0).astype(BF16)
            backs = jnp.where(causal, dot(gc_n, v_two, NT), 0.0).astype(BF16)
            w_rows = jnp.concatenate([weights[:, :CHUNK], weights[:, CHUNK:]], axis=0)
            b_rows = jnp.concatenate([backs[:, :CHUNK], backs[:, CHUNK:]], axis=0)
            sums = [
                dot(weights, v_two, NN),
                dot(backs, k_two, NN),
                dot(b_rows, q_two, TN),
                dot(w_rows, g_two, TN),
            ]
            if n:
                s = diagonal(state).astype(BF16)
                sums[0] = sums[0] + dot(qc_n, s, NN)
                sums[1] = sums[1] + dot(gc_n, s, NT)
            if n < CHUNKS - 1:
                r = diagonal(later[n]).astype(BF16)
                sums[2] = sums[2] + dot(v_n, r, NT)
                sums[3] = sums[3] + dot(k_n, r, NN)
                more = dot(k_n, v_n, TN)
                state = more if state is None else state + more
            for i, x in enumerate(sums):
                part[p, i, rows] = x
        return 0

    def entered(kind, p):
        rows = [back[kind, 2 * p], back[kind, 2 * p + 1]]
        return diagonal(jnp.concatenate(rows * 2, axis=0)).astype(BF16)

    def finish_states(p, _):
        at = lanes_of(p)
        s = entered(0, p)
        c = scale[...]
        attended[:, at] = (part[p, 0] + c * dot(q[:, at], s, NN)).astype(BF16)
        grad_q[:, at] = (part[p, 1] + c * dot(g[:, at], s, NT)).astype(BF16)
        return 0

    def finish_adjoints(p, _):
        at = lanes_of(p)
        r = entered(1, p)
        grad_k[:, at] = (part[p, 2] + dot(v[:, at], r, NT)).astype(BF16)
        grad_v[:, at] = (part[p, 3] + dot(k[:, at], r, NN)).astype(BF16)
        return 0

    lax.fori_loop(0, 5, inside, 0)
    add_column(0)
    lax.fori_loop(5, 8, inside, 0)
    add_column(1)
    add_plane(0)
    add_plane(1)
    for step in range(1, 16):
        returned(0, step, True).wait_recv()
    lax.fori_loop(0, PAIRS, finish_states, 0)
    for kind in range(2):
        for step in range(1, 16):
            forward(kind, step, False).wait_send()
            pl.when(ahead(kind, step))(across(kind, step, False).wait_send)
            returned(kind, step, False).wait_send()
    for step in range(1, 16):
        returned(1, step, True).wait_recv()
    lax.fori_loop(0, PAIRS, finish_adjoints, 0)


def store_kernel(*refs):
    sources, targets, sem = refs[:4], refs[4:8], refs[8]
    half = TOK // 2
    copies = [
        pltpu.make_async_copy(src.at[pl.ds(h * half, half)], dst.at[pl.ds(h * half, half)], sem.at[2 * i + h])
        for i, (src, dst) in enumerate(zip(sources, targets))
        for h in range(2)
    ]
    for copy in copies:
        copy.start()
    for copy in copies:
        copy.wait()


def on_device(queries, keys, values, cotangent):
    hbm = pl.BlockSpec(memory_space=pltpu.HBM)
    vmem = pl.BlockSpec(memory_space=pltpu.VMEM)
    dma = pltpu.SemaphoreType.DMA
    tokens = pltpu.VMEM((TOK, COLS), BF16)
    slices = pltpu.VMEM((2, 16, 32, 128), F32)
    results = pl.pallas_call(
        attention_kernel,
        name="attention",
        out_shape=(jax.ShapeDtypeStruct((TOK, COLS), BF16),) * 4,
        in_specs=[hbm] * 4,
        out_specs=(vmem,) * 4,
        scratch_shapes=[tokens] * 6
        + [
            pltpu.VMEM((TOK, 128), F32),
            pltpu.VMEM((PAIRS, 4, TOK, 128), F32),
            slices,
            slices,
            pltpu.VMEM((2, 32, 128), F32),
            slices,
            slices,
            slices,
            dma((4,)),
        ]
        + [dma((2, 16))] * 6,
        compiler_params=pltpu.CompilerParams(
            collective_id=0, has_side_effects=True, vmem_limit_bytes=40 << 20
        ),
    )(*(pltpu.with_memory_space_constraint(x, pltpu.HBM) for x in (queries, keys, values, cotangent)))
    return pl.pallas_call(
        store_kernel,
        name="store",
        out_shape=(jax.ShapeDtypeStruct((TOK, COLS), BF16),) * 4,
        in_specs=[pl.BlockSpec(memory_space=pl.ANY)] * 4,
        out_specs=(pl.BlockSpec(memory_space=pl.ANY),) * 4,
        scratch_shapes=[dma((8,))],
        compiler_params=pltpu.CompilerParams(vmem_limit_bytes=8 << 20),
    )(*results)


def solution(mesh):
    placed = P(("major", "minor"), None)
    return jax.shard_map(
        on_device, mesh=mesh, in_specs=(placed,) * 4, out_specs=(placed,) * 4, check_vma=False
    )
```

time: 56.1 us -> 46 us (0.82)
  Pallas kernels: 50.4 us -> 45.3 us
  local copies, waits for them, and re-layouts: 4.89 us -> 0 us
    pallas_call x2, Pallas kernels: 50.4 us -> 45.3 us  [the longest x1 43.2 us: on_device(): pl.pallas_call(attention_kernel, name='attention', out_shape=(jax.ShapeDt...]
    unnamed x8 -> x0, local copies, waits for them, and re-layouts: 4.89 us -> none
where the time goes in v2:
time: 46 us; the launch traced here: 45.9 us
  Pallas kernels  45.3 us (98%)
  between operations  0.64 us (1%)
    pallas_call x1, Pallas kernels, on_device(): pl.pallas_call(attention_kernel, name='attention', out_shape=(jax.ShapeDt...  43.2 us
    pallas_call x1, Pallas kernels, on_device(): pl.pallas_call(store_kernel, name='store', out_shape=(jax.ShapeDtypeStruc...  2.07 us

profile of v2, /device:TPU:1, one launch (start us, length us, event | category | flops | bytes accessed | tf_op | source)
XLA Modules:
  0.0 45.9 jit_solution(15754980712408615263)
XLA Ops:
  0.6 43.2 %attention.1 = (bf16[512,1024]{1,0:T(8,128)(2,1)S(1)}, bf16[512,1024]{1,0:T(8,128)(2,1)S(1)}, bf16[512,1024]{1,0:T(8,128)(2,1)S(1)}, bf16[512,1024]{1,0:T(8,128)(2,1)S(1)}) custom-call(bf16[512,1024]{1,0:T(8,128)(2,1)} %q_hbm.1, bf16[512,1024]{1,0:T(8,128)(2,1)} %k_hbm.1, bf16[512,1024]{1,0:T(8,128)(2,1)} %v_hbm.1, bf16[512,1024]{1,0:T(8,128)(2,1)} %g_hbm.1), custom_call_target="tpu_custom_call" | custom-call | tf_op jit(solution)/shard_map/attention/pallas_call | solution.py:287
  43.8 2.1 %store.1 = (bf16[512,1024]{1,0:T(8,128)(2,1)}, bf16[512,1024]{1,0:T(8,128)(2,1)}, bf16[512,1024]{1,0:T(8,128)(2,1)}, bf16[512,1024]{1,0:T(8,128)(2,1)}) custom-call(bf16[512,1024]{1,0:T(8,128)(2,1)S(1)} %get-tuple-element.8.refs_0_, bf16[512,1024]{1,0:T(8,128)(2,1)S(1)} %get-tuple-element.9.refs_1_, bf16[512,1024]{1,0:T(8,128)(2,1)S(1)} %get-tuple-element.10.refs_2_, ...), custom_call_target="tpu_custom_call" | custom-call | tf_op jit(solution)/shard_map/store/pallas_call | solution.py:310

commit v3 on v2

v3 whole, which is shorter than its diff:
```python
import jax
import jax.numpy as jnp
from jax import lax
from jax.experimental import pallas as pl
from jax.experimental.pallas import tpu as pltpu
from jax.sharding import PartitionSpec as P

TOK = 512
COLS = 1024
PAIRS = 8
CHUNK = 128
CHUNKS = TOK // CHUNK
F32 = jnp.float32
BF16 = jnp.bfloat16
MESH = pl.DeviceIdType.MESH

NT = (((1,), (1,)), ((), ()))
NN = (((1,), (0,)), ((), ()))
TN = (((0,), (0,)), ((), ()))


def dot(a, b, dims):
    return lax.dot_general(a, b, dims, preferred_element_type=F32)


def lanes_of(pair):
    return pl.ds(pl.multiple_of(pair * 128, 128), 128)


def token_scale(block, shape):
    pos = block * TOK + lax.broadcasted_iota(jnp.int32, shape, 0)
    return 1.0 / jnp.sqrt(pos.astype(F32) + 1.0)


def both_heads(x):
    low = lax.broadcasted_iota(jnp.int32, x.shape, 1) < 64
    zero = jnp.zeros_like(x)
    return jnp.concatenate([jnp.where(low, x, zero), jnp.where(low, zero, x)], axis=0)


def diagonal(x):
    row = lax.broadcasted_iota(jnp.int32, x.shape, 0) < 64
    col = lax.broadcasted_iota(jnp.int32, x.shape, 1) < 64
    return jnp.where(row == col, x, jnp.zeros_like(x))


def compact(x):
    low = lax.broadcasted_iota(jnp.int32, (64, 128), 1) < 64
    return jnp.where(low, x[0:64], x[64:128])


def attention_kernel(
    q_hbm, k_hbm, v_hbm, g_hbm, attended, grad_q, part_kv, k, v, adjoint,
    q, g, qc, scale, part, local, twin, low, both, f_low, f_both, total, plane, ret, back, other,
    in_sem, xs_sem, xr_sem, fs_sem, fr_sem, ps_sem, pr_sem, rs_sem, rr_sem, os_sem, or_sem,
):
    z = lax.axis_index("minor")
    group = lax.axis_index("major")
    core = lax.rem(group, 2)
    chip = group // 2
    zeros = jnp.zeros((32, 128), F32)
    sibling = {"minor": z, "major": chip * 2 + 1 - core}

    def up(step):
        return lax.rem(z + step, 8)

    def in_column(step):
        return {"minor": up(step), "major": group}

    def in_plane(step):
        return {"minor": z, "major": lax.rem(chip + step, 16) * 2 + core}

    loads = []
    for n, half in enumerate((1 - core, core)):
        cols = pl.ds(pl.multiple_of(half * 512, 512), 512)
        for m, (src, dst) in enumerate(((k_hbm, k), (v_hbm, v), (q_hbm, q), (g_hbm, g))):
            loads.append(pltpu.make_async_copy(src.at[:, cols], dst.at[:, cols], in_sem.at[n * 4 + m]))
    for n in (0, 1, 4, 5, 2, 3, 6, 7):
        loads[n].start()

    barrier = pltpu.get_barrier_semaphore()
    pl.semaphore_signal(barrier, inc=1, device_id=sibling, device_id_type=MESH)
    for step in range(1, 8):
        pl.semaphore_signal(barrier, inc=1, device_id=in_column(step), device_id_type=MESH)
    for step in range(1, 16):
        pl.semaphore_signal(barrier, inc=1, device_id=in_plane(step), device_id_type=MESH)

    def remote(src, dst, sent, landed, target):
        return pltpu.make_async_remote_copy(
            src_ref=src, dst_ref=dst, send_sem=sent, recv_sem=landed, device_id=target, device_id_type=MESH
        )

    def swap(kind):
        return remote(local.at[kind, 1 - core], twin.at[kind], xs_sem.at[kind], xr_sem.at[kind], sibling)

    def forward(kind, which, step, peer):
        src, dst = ((both, f_both), (low, f_low))[which]
        n = 2 * which + kind
        slot = up(step) if peer else z
        return remote(
            src.at[kind, up(step)], dst.at[kind, slot], fs_sem.at[n, step], fr_sem.at[n, slot], in_column(step)
        )

    def across(kind, step, peer):
        slot = lax.rem(chip + step, 16) if peer else chip
        return remote(
            total.at[kind], plane.at[kind, slot], ps_sem.at[kind, step], pr_sem.at[kind, slot], in_plane(step)
        )

    def returned(kind, step, peer):
        slot = up(step) if peer else z
        return remote(
            ret.at[kind, up(step)], back.at[kind, slot], rs_sem.at[kind, step], rr_sem.at[kind, slot], in_column(step)
        )

    def handed(kind, m):
        two = pl.ds(2 * m, 2)
        return remote(
            back.at[kind, two, 1 - core], other.at[kind, two], os_sem.at[kind, m], or_sem.at[kind, m], sibling
        )

    def ahead(kind, step):
        there = lax.rem(chip + step, 16)
        return there > chip if kind == 0 else there < chip

    def key_states(half):
        def body(m, _):
            at = lanes_of(half * 4 + m)
            s = compact(dot(k[:, at], v[:, at], TN))
            local[0, half, 2 * m] = s[0:32]
            local[0, half, 2 * m + 1] = s[32:64]
            return 0

        lax.fori_loop(0, 4, body, 0, unroll=True)

    def query_states(half):
        def body(m, _):
            at = lanes_of(half * 4 + m)
            scaled = (q[:, at].astype(F32) * scale[...]).astype(BF16)
            qc[:, at] = scaled
            r = compact(dot(scaled, g[:, at], TN))
            local[1, half, 2 * m] = r[0:32]
            local[1, half, 2 * m + 1] = r[32:64]
            return 0

        lax.fori_loop(0, 4, body, 0, unroll=True)

    def send_slices(kind):
        swap(kind).wait_recv()
        for j in range(8):
            own, theirs = local[kind, core, j], twin[kind, j]
            both[kind, j] = own + theirs
            low[kind, j] = jnp.where(core == 0, own, theirs)
        for step in range(1, 8):
            forward(kind, 0, step, False).start()
        f_both[kind, z] = both[kind, z]
        f_low[kind, z] = low[kind, z]

    def add_column(kind):
        for step in range(1, 8):
            forward(kind, 0, step, True).wait_recv()
        run = zeros
        for j in range(8):
            run = run + f_both[kind, j]
        total[kind] = run
        for step in range(1, 16):
            pl.when(ahead(kind, step))(across(kind, step, False).start)

    def add_blocks(kind):
        for step in range(1, 8):
            forward(kind, 1, step, True).wait_recv()
        order = list(range(8)) if kind == 0 else list(reversed(range(8)))
        run = zeros
        for part_of in (0, 1) if kind == 0 else (1, 0):
            for j in order:
                ret[kind, j, part_of] = run
                piece = f_low[kind, j]
                run = run + (piece if part_of == 0 else f_both[kind, j] - piece)

    def add_plane(kind):
        for step in range(1, 16):
            pl.when(ahead(1 - kind, step))(across(kind, step, True).wait_recv)
        entering = zeros
        for n in range(16):
            passed = n < chip if kind == 0 else n > chip
            entering = entering + jnp.where(passed, plane[kind, n], 0.0)
        for step in range(8):
            j = up(step)
            for part_of in range(2):
                ret[kind, j, part_of] = ret[kind, j, part_of] + entering
            if step:
                returned(kind, step, False).start()
        back[kind, z] = ret[kind, z]

    scale[...] = token_scale(group * 8 + z, (TOK, 128))
    for n in (0, 1, 4, 5):
        loads[n].wait()
    key_states(1 - core)
    key_states(core)
    for n in (2, 3, 6, 7):
        loads[n].wait()
    query_states(1 - core)
    query_states(core)
    pl.semaphore_wait(barrier, 23)
    swap(0).start()
    swap(1).start()
    send_slices(0)
    send_slices(1)
    for kind in range(2):
        for step in range(1, 8):
            forward(kind, 1, step, False).start()

    def inside(p, _):
        at = lanes_of(p)
        causal = lax.broadcasted_iota(jnp.int32, (CHUNK, 2 * CHUNK), 0) >= (
            lax.broadcasted_iota(jnp.int32, (CHUNK, 2 * CHUNK), 1) % CHUNK
        )
        state = None
        later = [None] * CHUNKS
        running = None
        for n in reversed(range(1, CHUNKS)):
            rows = pl.ds(n * CHUNK, CHUNK)
            more = dot(qc[rows, at], g[rows, at], TN)
            running = more if running is None else running + more
            later[n - 1] = running
        for n in range(CHUNKS):
            rows = pl.ds(n * CHUNK, CHUNK)
            q_n, k_n, v_n, g_n = q[rows, at], k[rows, at], v[rows, at], g[rows, at]
            qc_n = qc[rows, at]
            gc_n = (g_n.astype(F32) * scale[rows]).astype(BF16)
            k_two, v_two = both_heads(k_n), both_heads(v_n)
            q_two, g_two = both_heads(q_n), both_heads(g_n)
            weights = jnp.where(causal, dot(qc_n, k_two, NT), 0.0).astype(BF16)
            backs = jnp.where(causal, dot(gc_n, v_two, NT), 0.0).astype(BF16)
            w_rows = jnp.concatenate([weights[:, :CHUNK], weights[:, CHUNK:]], axis=0)
            b_rows = jnp.concatenate([backs[:, :CHUNK], backs[:, CHUNK:]], axis=0)
            sums = [
                dot(weights, v_two, NN),
                dot(backs, k_two, NN),
                dot(b_rows, q_two, TN),
                dot(w_rows, g_two, TN),
            ]
            if n:
                s = diagonal(state).astype(BF16)
                sums[0] = sums[0] + dot(qc_n, s, NN)
                sums[1] = sums[1] + dot(gc_n, s, NT)
            if n < CHUNKS - 1:
                r = diagonal(later[n]).astype(BF16)
                sums[2] = sums[2] + dot(v_n, r, NT)
                sums[3] = sums[3] + dot(k_n, r, NN)
                more = dot(k_n, v_n, TN)
                state = more if state is None else state + more
            for i, x in enumerate(sums):
                if i < 2:
                    part[p, i, rows] = x
                else:
                    part_kv[p, i - 2, rows] = x
        return 0


    def finish(kind, p, rows):
        if kind == 0:
            at = lanes_of(p)
            x = diagonal(jnp.concatenate(rows * 2, axis=0)).astype(BF16)
            c = scale[...]
            attended[:, at] = (part[p, 0] + c * dot(q[:, at], x, NN)).astype(BF16)
            grad_q[:, at] = (part[p, 1] + c * dot(g[:, at], x, NT)).astype(BF16)
        else:
            adjoint[p, 0:32] = rows[0]
            adjoint[p, 32:64] = rows[1]

    def turn(i):
        return lax.rem(z // 2 + i + i // 2 - 2 * (i // 3), 4)

    def arrived(kind, j):
        step = lax.rem(j - z + 8, 8)
        pl.when(j != z)(returned(kind, step, True).wait_recv)

    def finish_own(kind):
        def body(i, _):
            m = turn(i)
            arrived(kind, 2 * m)
            arrived(kind, 2 * m + 1)
            handed(kind, m).start()
            finish(kind, core * 4 + m, [back[kind, 2 * m, core], back[kind, 2 * m + 1, core]])
            return 0

        lax.fori_loop(0, 4, body, 0)

    def finish_other(kind):
        def body(i, _):
            m = turn(i)
            handed(kind, m).wait_recv()
            finish(kind, (1 - core) * 4 + m, [other[kind, 2 * m], other[kind, 2 * m + 1]])
            return 0

        lax.fori_loop(0, 4, body, 0)

    lax.fori_loop(0, 3, inside, 0)
    add_column(0)
    add_column(1)
    lax.fori_loop(3, 5, inside, 0)
    add_blocks(0)
    add_blocks(1)
    add_plane(0)
    add_plane(1)
    lax.fori_loop(5, 8, inside, 0)
    finish_own(0)
    finish_other(0)
    for kind in range(2):
        swap(kind).wait_send()
        for step in range(1, 8):
            forward(kind, 0, step, False).wait_send()
            forward(kind, 1, step, False).wait_send()
            returned(kind, step, False).wait_send()
        for step in range(1, 16):
            pl.when(ahead(kind, step))(across(kind, step, False).wait_send)
    finish_own(1)
    finish_other(1)
    for kind in range(2):
        for m in range(4):
            handed(kind, m).wait_send()


def store_kernel(attended, grad_q, part_kv, k, v, adjoint, a_hbm, q_hbm, k_hbm, v_hbm, k_out, v_out, sem, kv_sem):
    half = TOK // 2
    copies = [
        pltpu.make_async_copy(src.at[pl.ds(h * half, half)], dst.at[pl.ds(h * half, half)], sem.at[2 * i + h])
        for i, (src, dst) in enumerate(((attended, a_hbm), (grad_q, q_hbm)))
        for h in range(2)
    ]
    for copy in copies:
        copy.start()
    for p in range(PAIRS):
        at = pl.ds(p * 128, 128)
        x = diagonal(jnp.concatenate([adjoint[p]] * 2, axis=0)).astype(BF16)
        k_out[:, at] = (part_kv[p, 0] + dot(v[:, at], x, NT)).astype(BF16)
        v_out[:, at] = (part_kv[p, 1] + dot(k[:, at], x, NN)).astype(BF16)
        if p % 2:
            cols = pl.ds(p * 128 - 128, 256)
            for i, (src, dst) in enumerate(((k_out, k_hbm), (v_out, v_hbm))):
                copies.append(pltpu.make_async_copy(src.at[:, cols], dst.at[:, cols], kv_sem.at[i, p // 2]))
                copies[-1].start()
    for copy in copies:
        copy.wait()


def on_device(queries, keys, values, cotangent):
    hbm = pl.BlockSpec(memory_space=pltpu.HBM)
    vmem = pl.BlockSpec(memory_space=pltpu.VMEM)
    anywhere = pl.BlockSpec(memory_space=pl.ANY)
    dma = pltpu.SemaphoreType.DMA
    tokens = pltpu.VMEM((TOK, COLS), BF16)
    out = jax.ShapeDtypeStruct((TOK, COLS), BF16)

    def slices(*lead):
        return pltpu.VMEM((*lead, 32, 128), F32)

    results = pl.pallas_call(
        attention_kernel,
        name="attention",
        out_shape=(
            out,
            out,
            jax.ShapeDtypeStruct((PAIRS, 2, TOK, 128), F32),
            out,
            out,
            jax.ShapeDtypeStruct((PAIRS, 64, 128), F32),
        ),
        in_specs=[hbm] * 4,
        out_specs=(vmem,) * 6,
        scratch_shapes=[tokens] * 3
        + [
            pltpu.VMEM((TOK, 128), F32),
            pltpu.VMEM((PAIRS, 2, TOK, 128), F32),
            slices(2, 2, 8),
            slices(2, 8),
            slices(2, 8),
            slices(2, 8),
            slices(2, 8),
            slices(2, 8),
            slices(2),
            slices(2, 16),
            slices(2, 8, 2),
            slices(2, 8, 2),
            slices(2, 8),
            dma((8,)),
            dma((2,)),
            dma((2,)),
            dma((4, 8)),
            dma((4, 8)),
            dma((2, 16)),
            dma((2, 16)),
            dma((2, 8)),
            dma((2, 8)),
            dma((2, 4)),
            dma((2, 4)),
        ],
        compiler_params=pltpu.CompilerParams(
            collective_id=0, has_side_effects=True, vmem_limit_bytes=32 << 20
        ),
    )(*(pltpu.with_memory_space_constraint(x, pltpu.HBM) for x in (queries, keys, values, cotangent)))
    return pl.pallas_call(
        store_kernel,
        name="store",
        out_shape=(out,) * 4,
        in_specs=[anywhere] * 2 + [vmem] * 4,
        out_specs=(anywhere,) * 4,
        scratch_shapes=[tokens, tokens, dma((4,)), dma((2, 4))],
        compiler_params=pltpu.CompilerParams(vmem_limit_bytes=16 << 20),
    )(*results)


def solution(mesh):
    placed = P(("major", "minor"), None)
    return jax.shard_map(
        on_device, mesh=mesh, in_specs=(placed,) * 4, out_specs=(placed,) * 4, check_vma=False
    )
```

time: 46 us -> 45.4 us (0.987)
  Pallas kernels: 45.3 us -> 44.7 us
    pallas_call x2, Pallas kernels: 45.3 us -> 44.7 us  [the longest x1 42.3 us: on_device(): pl.pallas_call(attention_kernel, name='attention', out_shape=(out, out, j...]
where the time goes in v3:
time: 45.4 us
  Pallas kernels  44.7 us (98%)
  between operations  0.64 us (1%)
    pallas_call x1, Pallas kernels, on_device(): pl.pallas_call(attention_kernel, name='attention', out_shape=(out, out, j...  42.3 us
    pallas_call x1, Pallas kernels, on_device(): pl.pallas_call(store_kernel, name='store', out_shape=(out,) * 4, in_specs...  2.43 us

profile of v3, /device:TPU:1, one launch (start us, length us, event | category | flops | bytes accessed | tf_op | source)
XLA Modules:
  0.0 45.4 jit_solution(7072387616747787325)
XLA Ops:
  0.6 42.3 %attention.1 = (bf16[512,1024]{1,0:T(8,128)(2,1)S(1)}, bf16[512,1024]{1,0:T(8,128)(2,1)S(1)}, f32[8,2,512,128]{3,2,1,0:T(8,128)S(1)}, bf16[512,1024]{1,0:T(8,128...) custom-call(bf16[512,1024]{1,0:T(8,128)(2,1)} %q_hbm.1, bf16[512,1024]{1,0:T(8,128)(2,1)} %k_hbm.1, ...), custom_call_target="tpu_custom_call" | custom-call | tf_op jit(solution)/shard_map/attention/pallas_call | solution.py:359
  42.9 2.4 %store.1 = (bf16[512,1024]{1,0:T(8,128)(2,1)}, bf16[512,1024]{1,0:T(8,128)(2,1)}, bf16[512,1024]{1,0:T(8,128)(2,1)}, bf16[512,1024]{1,0:T(8,128)(2,1)}) custom-call(bf16[512,1024]{1,0:T(8,128)(2,1)S(1)} %get-tuple-element.10.attended, bf16[512,1024]{1,0:T(8,128)(2,1)S(1)} %get-tuple-element.11.grad_q, f32[8,2,512,128]{3,2,1,0:T(8,128)S(1)} %get-tuple-element.12.part_kv, ...), custom_call_target="tpu_custom_call" | custom-call | tf_op jit(solution)/shard_map/store/pallas_call | solution.py:403
